TPU v7x, 32 devices: a whole 2x2x4 slice. The times are simulated.
32 devices in a mesh: groups: 2 (over y), row: 4 (over x, core), col: 4 (over z).
Axes of the slice: x: 2, y: 2, z: 4, core: 2. Of those that a mesh axis runs over, the one named last changes fastest.
Arguments:
- slope_matrix: bfloat16 [1024, 1024], P(('groups', 'row'), 'col'), parts along dimension 0, may hold values from -0.3125 to 0.3125
- prior_matrix: bfloat16 [1024, 1024], P(('groups', 'row'), 'col'), parts along dimension 0, may hold values from -0.3125 to 0.3125
- slope_blocks: int32 [8, 8], P(('groups', 'row'), 'col'), parts along dimension 0, may hold values from 0 to 23, as said below
- prior_blocks: int32 [8, 8], P(('groups', 'row'), 'col'), parts along dimension 0, may hold values from 0 to 23, as said below
- weight_ids: int32 [512], P(('groups', 'row')), parts along dimension 0, may hold values from 0 to 15
- valid_mask: int32 [512], P(('groups', 'row')), parts along dimension 0, may hold values 0 or 1
- noise_weights: float32 [32], P('groups'), parts along dimension 0, may hold values from 0.25 to 4
- prior_weights: bfloat16 [1024], P(('groups', 'row')), parts along dimension 0, may hold values from 0.19921875 to 2
- frames: float32 [6144, 64], P(('groups', 'row', 'col')), parts along dimension 0, may hold values from -6 to 6
Outputs:
- gram_matrix: float32 [6144, 3072], P(('groups', 'row'), 'col'), parts along dimension 0
- applied: float32 [6144, 64], P(('groups', 'row', 'col')), parts along dimension 0
There are 2 independent parts, one for each index of `groups`. A program takes and returns all parts, laid end to end along the dimension named above; each array names one. Nothing has to cross between parts.
Inputs may be any that keep to these rules, and one draw needn't show every extreme that they name: `slope_blocks`: row i names, for each block-column set c (entries c * 2 to c * 2 + 1), 2 distinct actuator blocks of that set, c * 6 to c * 6 + 5, in the order in which their blocks are stored. `prior_blocks`: row i names, for each block-column set c (entries c * 2 to c * 2 + 1), 2 distinct actuator blocks of that set, c * 6 to c * 6 + 5, in the order in which their blocks are stored.
All inputs are finite; a program needn't handle non-finite values. No bound on the sum of `valid_mask` on one device may be relied on, other than what follows from the above.
Results may differ from a plain program's by a relative error of at most 0.007.
Values may be sent and summed in bfloat16 or wider, within the bound.
A program may use at most 128 MiB of HBM per device.

v0:
```python
import jax
import jax.numpy as jnp
from jax import lax
from jax.sharding import PartitionSpec as P

BS = 128
AB = 6


def from_root(block, axis, owner):
    block = jnp.where(lax.axis_index(axis) == owner, block, jnp.zeros_like(block))
    return lax.psum(block, axis)


def expand_blocks(values, block_ids, set_index):
    block_count = block_ids.shape[0]
    chosen = block_ids.shape[1]
    targets = set_index * AB + jnp.arange(AB, dtype=jnp.int32)
    onehot = (block_ids[:, :, None] == targets[None, None, :]).astype(jnp.bfloat16)
    shaped = values.reshape(block_count, BS, chosen, BS)
    expanded = jnp.einsum("rskb,rka->rsab", shaped, onehot, preferred_element_type=jnp.float32)
    return expanded.astype(jnp.bfloat16).reshape(block_count * BS, AB * BS)


def shards(
    slope_matrix,
    prior_matrix,
    slope_blocks,
    prior_blocks,
    weight_ids,
    valid_mask,
    noise_weights,
    prior_weights,
    frames,
):
    row_index = lax.axis_index("row")
    col_index = lax.axis_index("col")
    classes = jnp.arange(noise_weights.shape[0], dtype=jnp.int32)
    picked = jnp.sum(
        jnp.where(weight_ids[:, None] == classes[None, :], noise_weights[None, :], 0.0), axis=1
    )
    subap_weight = picked * valid_mask.astype(jnp.float32)
    slope_weight = jnp.repeat(subap_weight, 2).astype(jnp.bfloat16)
    local_rows = jnp.concatenate([slope_matrix, prior_matrix], axis=0)
    local_ids = jnp.concatenate([slope_blocks, prior_blocks], axis=0)
    local_weight = jnp.concatenate([slope_weight, prior_weights], axis=0)
    all_rows, all_ids, all_weight = (
        lax.all_gather(local_rows, "row", axis=0, tiled=True),
        lax.all_gather(local_ids, "row", axis=0, tiled=True),
        lax.all_gather(local_weight, "row", axis=0, tiled=True),
    )
    row_scale = all_weight.astype(jnp.float32)[:, None]
    weighted_rows = (all_rows.astype(jnp.float32) * row_scale).astype(jnp.bfloat16)
    weighted_cols = expand_blocks(weighted_rows, all_ids, col_index)
    sent_rows, sent_ids = (
        from_root(all_rows, "col", row_index),
        from_root(all_ids, "col", row_index),
    )
    row_dense = expand_blocks(sent_rows, sent_ids, row_index)
    gram_tile = lax.dot_general(
        row_dense, weighted_cols, (((0,), (0,)), ((), ())), preferred_element_type=jnp.float32
    )
    frames_rows = lax.all_gather(frames, "col", axis=0, tiled=True)
    frames_cols = from_root(frames_rows, "row", col_index)
    partial_image = jnp.dot(
        gram_tile, frames_cols, precision=lax.Precision.HIGHEST, preferred_element_type=jnp.float32
    )
    applied = lax.psum_scatter(partial_image, "col", scatter_dimension=0, tiled=True)
    return (gram_tile, applied)


def solution(mesh):
    in_specs = (
        P(("groups", "row"), "col"),
        P(("groups", "row"), "col"),
        P(("groups", "row"), "col"),
        P(("groups", "row"), "col"),
        P(("groups", "row")),
        P(("groups", "row")),
        P("groups"),
        P(("groups", "row")),
        P(("groups", "row", "col"), None),
    )
    out_specs = (P(("groups", "row"), "col"), P(("groups", "row", "col"), None))
    return jax.shard_map(shards, mesh=mesh, in_specs=in_specs, out_specs=out_specs, check_vma=False)
```

profile of v0, /device:TPU:0, one launch (start us, length us, event | category | flops | bytes accessed | tf_op | source)
XLA Modules:
  0.0 125.8 jit_solution(12584636910592303553)
XLA Ops:
  7.2 0.0 all-reduce.3.cloned.1.call-start
  7.2 0.9 pad_maximum_fusion
  8.1 8.6 %all_gather.13 = bf16[1024,256]{1,0:T(8,128)(2,1)S(1)} all-gather(bf16[256,256]{1,0:T(8,128)(2,1)S(1)} %pad_maximum_fusion), channel_id=1, replica_groups=mesh['groups'=2,'row'=4,'col'=4] {'row'}, dimensions={0}, use_global_device_ids=true | all-gather | bytes 655360 | tf_op jit(solution)/shard_map/all_gather | solution.py:48
  16.8 0.0 copy-start.8
  16.8 0.9 reshape.31
  17.7 0.0 all-reduce.3.cloned.1.call-update
  17.7 0.0 all-reduce.5.cloned.1.call-start
  17.8 15.8 %all-gather.2 = f32[4,192,64]{1,2,0:T(8,128)S(1)} all-gather(f32[1,192,64]{1,2,0:T(8,128)S(1)} %bitcast.36), channel_id=1, replica_groups=mesh['groups'=2,'row'=4,'col'=4] {'col'}, dimensions={0}, use_global_device_ids=true | all-gather | bytes 245760 | tf_op jit(solution)/shard_map/all_gather | solution.py:63
  33.6 0.2 copy.31
  33.8 0.9 reshape.44
  34.7 0.0 all-reduce.5.cloned.1.call-update
  34.7 0.0 reduce-scatter.4.cloned.1.call-start
  34.8 5.1 %all-gather = s32[4,2,2]{2,1,0:T(2,128)S(1)} all-gather(s32[1,2,2]{2,1,0:T(2,128)S(1)} %add_bitcast_fusion), channel_id=1, replica_groups=mesh['groups'=2,'row'=4,'col'=4] {'row'}, dimensions={0}, use_global_device_ids=true | all-gather | bytes 80 | tf_op jit(solution)/shard_map/all_gather | solution.py:49
  39.8 0.1 copy.34
  39.9 7.8 %psum.21 = s32[8,2]{0,1:T(2,128)S(1)} all-reduce(s32[8,2]{0,1:T(2,128)S(1)} %broadcast_select_fusion.2), channel_id=1, replica_groups=mesh['groups'=2,'row'=4,'col'=4] {'col'}, use_global_device_ids=true, to_apply=%region_0.1 | all-reduce | flops 16 | bytes 128 | tf_op jit(solution)/shard_map/psum | solution.py:12
  47.7 0.1 copy.27
  47.8 0.1 select_reduce_fusion
  47.9 0.1 broadcast_in_dim.32
  48.0 0.2 convert_element_type.38
  48.2 5.1 %all-gather.1 = bf16[4,1,256]{2,1,0:T(2,128)(2,1)S(1)} all-gather(bf16[1,1,256]{2,1,0:T(2,128)(2,1)S(1)} %reshape.37), channel_id=1, replica_groups=mesh['groups'=2,'row'=4,'col'=4] {'row'}, dimensions={0}, use_global_device_ids=true | all-gather | bytes 2560 | tf_op jit(solution)/shard_map/all_gather | solution.py:50
  53.3 0.2 multiply_convert_fusion
  53.5 0.1 reshape.33
  53.6 2.2 %convolution_convert_fusion = bf16[8,6,128,128]{3,1,2,0:T(8,128)(2,1)} fusion(bf16[8,128,2,128]{3,2,1,0:T(2,128)(2,1)S(1)} %reshape.33, s32[6]{0:T(128)S(1)} %iota_add_fusion, s32[8,2]{1,0:T(8,128)S(1)} %bitcast.38), kind=kOutput, calls=%fused_computation | convolution fusion | flops 3932256 | bytes 2097240 | tf_op jit(solution)/shard_map/rskb,rka->rsab/dot_general | solution.py:21
  55.8 3.4 %all-reduce.3.cloned.1.call-done = bf16[8,128,2,128]{3,2,1,0:T(2,128)(2,1)} async-done(((bf16[8,128,2,128]{3,2,1,0:T(2,128)(2,1)}), bf16[8,128,2,128]{3,2,1,0:T(2,128)(2,1)}) %all-reduce.3.cloned.1.call-update) | async-done | bytes 524304 | tf_op jit(solution)/shard_map/psum | solution.py:12
  59.2 2.1 %convolution_convert_fusion.1 = bf16[8,6,128,128]{3,1,2,0:T(8,128)(2,1)S(1)} fusion(bf16[8,128,2,128]{3,2,1,0:T(2,128)(2,1)} %all-reduce.3.cloned.1.call-done, s32[6]{0:T(128)S(1)} %iota_add_fusion.1, s32[8,2]{1,0:T(8,128)S(1)} %copy.27), kind=kOutput, calls=%fused_computation.1 | convolution fusion | flops 3932256 | bytes 2097240 | tf_op jit(solution)/shard_map/rskb,rka->rsab/dot_general | solution.py:21
  61.3 1.5 %fusion = f32[768,768]{1,0:T(8,128)S(1)} fusion(bf16[128,8,6,128]{3,2,1,0:T(8,128)(2,1)S(1)} %bitcast.34, bf16[128,8,6,128]{3,2,1,0:T(8,128)(2,1)S(1)} %bitcast.35), kind=kOutput, calls=%fused_computation.2 | convolution fusion | flops 1207959552 | bytes 5505024 | tf_op jit(solution)/shard_map/dot_general | solution.py:60
  62.8 0.0 copy-start
  62.8 30.4 %all-reduce.5.cloned.1.call-done = f32[768,64]{0,1:T(8,128)} async-done(((f32[768,64]{0,1:T(8,128)}), f32[768,64]{0,1:T(8,128)}) %all-reduce.5.cloned.1.call-update) | async-done | bytes 196624 | tf_op jit(solution)/shard_map/psum | solution.py:12
  93.2 3.7 %fusion.13 = f32[768,64]{1,0:T(8,128)} fusion(f32[768,768]{1,0:T(8,128)S(1)} %fusion, f32[768,64]{0,1:T(8,128)} %all-reduce.5.cloned.1.call-done), kind=kOutput, calls=%fused_computation.27 | convolution fusion | flops 452984832 | bytes 2752512
  96.8 0.0 reduce-scatter.4.cloned.1.call-update
  96.9 20.8 %reduce-scatter.4.cloned.1.call-done = f32[192,64]{1,0:T(8,128)} async-done(((f32[768,64]{1,0:T(8,128)}), f32[192,64]{1,0:T(8,128)}) %reduce-scatter.4.cloned.1.call-update) | async-done | bytes 49168
  117.6 1.6 %copy.38 = f32[192,64]{0,1:T(8,128)} copy(f32[192,64]{1,0:T(8,128)} %reduce-scatter.4.cloned.1.call-done) | data formatting | bytes 98304
  (26 shorter events, 0.1 us)
Async XLA Ops:
  7.2 10.6 %copy-start.2 = (f32[192,64]{0,1:T(8,128)S(1)}, f32[192,64]{0,1:T(8,128)}, u32[]{:S(2)}) copy-start(f32[192,64]{0,1:T(8,128)} %param.17) | copy-start | bytes 147460
  7.2 52.0 %all-reduce.3.cloned.1.call-start = ((), (), s32[]{:S(2)}) async-start(), calls=%async_computation.1 | async-start | bytes 1048576 | tf_op jit(solution)/shard_map/psum | solution.py:12
  16.7 18.0 %copy-start.3 = (s32[1,2]{1,0:T(1,128)S(1)}, s32[1,2]{1,0:T(1,128)}, u32[]{:S(2)}) copy-start(s32[1,2]{1,0:T(1,128)} %param.12) | copy-start | bytes 28
  16.7 18.0 %copy-start.4 = (s32[1,2]{1,0:T(1,128)S(1)}, s32[1,2]{1,0:T(1,128)}, u32[]{:S(2)}) copy-start(s32[1,2]{1,0:T(1,128)} %param.11) | copy-start | bytes 28
  16.7 31.1 %copy-start.5 = (f32[16]{0:T(128)S(1)}, f32[16]{0:T(128)}, u32[]{:S(2)}) copy-start(f32[16]{0:T(128)} %param.15) | copy-start | bytes 196
  16.7 31.1 %copy-start.6 = (s32[64]{0:T(128)S(1)}, s32[64]{0:T(128)}, u32[]{:S(2)}) copy-start(s32[64]{0:T(128)} %param.13) | copy-start | bytes 772
  16.7 31.2 %copy-start.7 = (s32[64]{0:T(128)S(1)}, s32[64]{0:T(128)}, u32[]{:S(2)}) copy-start(s32[64]{0:T(128)} %param.14) | copy-start | bytes 772
  16.8 31.3 %copy-start.8 = (bf16[128]{0:T(256)(128)(2,1)S(1)}, bf16[128]{0:T(256)(128)(2,1)}, u32[]{:S(2)}) copy-start(bf16[128]{0:T(256)(128)(2,1)} %param.16) | copy-start | bytes 772
  17.7 75.4 %all-reduce.5.cloned.1.call-start = ((), (), s32[]{:S(2)}) async-start(), calls=%async_computation.2 | async-start | bytes 393216 | tf_op jit(solution)/shard_map/psum | solution.py:12
  34.7 82.9 %reduce-scatter.4.cloned.1.call-start = ((), (), s32[]{:S(2)}) async-start(), calls=%async_computation.3 | async-start | bytes 491520
  59.2 2.1 %copy-start.1 = (bf16[8,6,128,128]{3,1,2,0:T(8,128)(2,1)S(1)}, bf16[8,6,128,128]{3,1,2,0:T(8,128)(2,1)}, u32[]{:S(2)}) copy-start(bf16[8,6,128,128]{3,1,2,0:T(8,128)(2,1)} %convolution_convert_fusion) | copy-start | bytes 4718596
  62.8 56.5 %copy-start = (f32[768,768]{1,0:T(8,128)}, f32[768,768]{1,0:T(8,128)S(1)}, u32[]{:S(2)}) copy-start(f32[768,768]{1,0:T(8,128)S(1)} %fusion) | copy-start | bytes 7077892
Sparse Core Ops, SparseCore 0:
  17.9 41.2 all-reduce.2
  61.5 31.6 all-reduce.4
  97.0 20.5 reduce-scatter.3
where the time goes:
time: 126 us
  waiting for transfers between devices  54.6 us (43%)
  blocking collectives  42.3 us (34%)
  between operations  13.9 us (11%)
  matrix products  9.43 us (7%)
  local copies, waits for them, and re-layouts  4.09 us (3%)
  other arithmetic  1.28 us (1%)
    psum x2, waiting for transfers between devices, from_root(): return lax.psum(block, axis)  33.8 us
    unnamed x4, waiting for transfers between devices  20.8 us
    all_gather x1, blocking collectives, shards(): frames_rows = lax.all_gather(frames, 'col', axis=0, tiled=True)  15.8 us
    all_gather x1, blocking collectives, shards(): lax.all_gather(local_rows, 'row', axis=0, tiled=True)  8.62 us
    psum x1, blocking collectives, from_root(): return lax.psum(block, axis)  7.77 us
    all_gather x1, blocking collectives, shards(): lax.all_gather(local_weight, 'row', axis=0, tiled=True)  5.07 us
    all_gather x1, blocking collectives, shards(): lax.all_gather(local_ids, 'row', axis=0, tiled=True)  5.07 us
    dot_general x2, matrix products, expand_blocks(): jnp.einsum('rskb,rka->rsab', shaped, onehot, preferred_element_type=jnp.f...  4.3 us
  transfers between devices with their start and end apart: 3, of which 3 were waited for; matrix products, arithmetic and copies ran while one was open for 6% of the time, Pallas kernels for 0%

commit v1 on v0

v1 whole, which is shorter than its diff:
```python
import functools

import jax
import jax.numpy as jnp
from jax import lax
from jax.experimental import pallas as pl
from jax.experimental.pallas import tpu as pltpu
from jax.sharding import PartitionSpec as P

BS = 128
AB = 6
EXTRA = 16
MESH = pl.DeviceIdType.MESH


def remote(src, dst, send, recv, axis, to):
    return pltpu.make_async_remote_copy(
        src_ref=src, dst_ref=dst, send_sem=send, recv_sem=recv,
        device_id={axis: to}, device_id_type=MESH,
    )


def exchange(
    n, ids_ref, slope_ref, prior_ref, extra_ref, frames_ref,
    blocks, images,
    held, own_frames, set_frames, partial,
    send_z, recv_z, send_c, recv_c, send_r, recv_r,
    send_p, recv_p, send_f, recv_f, send_v, recv_v, send_u, recv_u,
):
    row = lax.axis_index("row")
    col = lax.axis_index("col")
    rows = slope_ref.shape[0]
    piece = own_frames.shape[0]
    barrier = pltpu.get_barrier_semaphore()
    for t in range(1, n):
        pl.semaphore_signal(barrier, inc=1, device_id={"col": lax.rem(col + t, n)}, device_id_type=MESH)
        pl.semaphore_signal(barrier, inc=1, device_id={"row": lax.rem(row + t, n)}, device_id_type=MESH)
    own_frames[...] = frames_ref[...].astype(jnp.bfloat16)
    held[col, pl.ds(0, rows), :] = slope_ref[...]
    held[col, pl.ds(rows, rows), :] = prior_ref[...]
    held[col, pl.ds(2 * rows, EXTRA), :] = extra_ref[...]
    pl.semaphore_wait(barrier, 2 * (n - 1))

    def frame_piece(source):
        return remote(
            own_frames, set_frames.at[pl.ds(source * piece, piece), :],
            send_p, recv_p.at[source], "col", row,
        )

    @pl.when(row != col)
    def _():
        frame_piece(col).start()

    sends_z = []
    for t in range(1, n):
        copy = remote(
            held.at[col], held.at[col], send_z.at[t - 1], recv_z.at[t - 1], "col", lax.rem(col + t, n)
        )
        copy.start()
        sends_z.append(copy)
    sends_c = []
    for s in range(1, n):
        copy = remote(
            held.at[col], blocks.at[0, row], send_c.at[s - 1], recv_c.at[s - 1], "row", lax.rem(row + s, n)
        )
        copy.start()
        sends_c.append(copy)
    blocks[0, row] = held[col]

    def whole_frames(s):
        return remote(
            set_frames, set_frames, send_f.at[s - 1], recv_f, "row", lax.rem(row + s, n)
        )

    @pl.when(row == col)
    def _():
        set_frames[pl.ds(col * piece, piece), :] = own_frames[...]
        for t in range(1, n):
            frame_piece(lax.rem(col + t, n)).wait_recv()
        for s in range(1, n):
            whole_frames(s).start()

    @pl.when(row != col)
    def _():
        whole_frames(1).wait_recv()

    parts = []
    for part, ref in enumerate((slope_ref, prior_ref)):
        total = jnp.zeros((rows, set_frames.shape[1]), jnp.float32)
        for k in range(ref.shape[1] // BS):
            wanted = jnp.full((BS, set_frames.shape[1]), ids_ref[part * (ref.shape[1] // BS) + k], jnp.int32)
            chosen = jnp.zeros(wanted.shape, jnp.float32)
            for a in range(AB):
                block = set_frames[a * BS:(a + 1) * BS, :].astype(jnp.float32)
                chosen = jnp.where(wanted == a, block, chosen)
            total += jnp.dot(
                ref[:, k * BS:(k + 1) * BS], chosen.astype(jnp.bfloat16),
                preferred_element_type=jnp.float32,
            )
        parts.append(total)
    partial[col] = jnp.concatenate(parts, axis=1).astype(jnp.bfloat16)
    sends_v = []
    for t in range(1, n):
        copy = remote(
            partial.at[col], partial.at[col], send_v.at[t - 1], recv_v.at[t - 1], "col", lax.rem(col + t, n)
        )
        copy.start()
        sends_v.append(copy)

    def forward(t):
        source = lax.rem(col + n - t, n)
        return remote(
            held.at[source], blocks.at[1, row], send_r.at[t - 1],
            recv_r.at[lax.rem(source + n - row, n)], "row", source,
        )

    for t in range(1, n):
        sends_z[t - 1].wait_recv()
        source = lax.rem(col + n - t, n)

        @pl.when(source == row)
        def _():
            blocks[1, row] = held[row]

        @pl.when(source != row)
        def _():
            forward(t).start()

    for copy in sends_v:
        copy.wait_recv()
    image = partial[0].astype(jnp.float32)
    for t in range(1, n):
        image += partial[t].astype(jnp.float32)
    images[row] = image.astype(jnp.bfloat16)
    sends_u = []
    for s in range(1, n):
        copy = remote(
            images.at[row], images.at[row], send_u.at[s - 1], recv_u.at[s - 1], "row", lax.rem(row + s, n)
        )
        copy.start()
        sends_u.append(copy)

    for copy in sends_c:
        copy.wait_recv()

    @pl.when(row != col)
    def _():
        for s in range(1, n):
            source = lax.rem(row + n - s, n)
            remote(
                held.at[0], blocks.at[1, source], send_r.at[0], recv_r.at[s], "row", source
            ).wait_recv()
        frame_piece(col).wait_send()

    @pl.when(row == col)
    def _():
        for s in range(1, n):
            whole_frames(s).wait_send()

    for copy in sends_u:
        copy.wait_recv()
    for t in range(1, n):

        @pl.when(lax.rem(col + n - t, n) != row)
        def _():
            forward(t).wait_send()

    for copy in sends_z + sends_c + sends_v + sends_u:
        copy.wait_send()


def combine(n, ids_ref, blocks, images, gram, applied, total):
    rows = images.shape[1]
    kept = blocks.shape[3] // BS
    wide = images.shape[2] // 2
    same = ids_ref[4 * n * kept]
    quarter = ids_ref[4 * n * kept + 1]
    gram[...] = jnp.zeros_like(gram)
    total[...] = jnp.zeros_like(total)
    for i in range(n):
        for part in range(2):
            left = blocks[same, i, part * rows:(part + 1) * rows, :]
            right = blocks[0, i, part * rows:(part + 1) * rows, :].astype(jnp.float32)
            weight = blocks[0, i, 2 * rows:2 * rows + EXTRA, part * rows:(part + 1) * rows]
            weight = weight.astype(jnp.float32)[1:2, :]
            weight = jnp.transpose(jnp.broadcast_to(weight, (BS, rows)))
            right = jnp.concatenate(
                [right[:, k * BS:(k + 1) * BS] * weight for k in range(kept)], axis=1
            ).astype(jnp.bfloat16)
            image = images[i, :, part * wide:(part + 1) * wide].astype(jnp.float32)
            image = (image * weight[:, :wide]).astype(jnp.bfloat16)
            over = (((0,), (0,)), ((), ()))
            product = lax.dot_general(left, right, over, preferred_element_type=jnp.float32)
            shown = lax.dot_general(left, image, over, preferred_element_type=jnp.float32)
            for a in range(kept):
                down = ids_ref[(same * n + i) * 2 * kept + part * kept + a]
                down = pl.multiple_of(down * BS, BS)
                total[pl.ds(down, BS), :] += shown[a * BS:(a + 1) * BS]
                for b in range(kept):
                    across = ids_ref[i * 2 * kept + part * kept + b]
                    across = pl.multiple_of(across * BS, BS)
                    gram[pl.ds(down, BS), pl.ds(across, BS)] += product[
                        a * BS:(a + 1) * BS, b * BS:(b + 1) * BS
                    ]
    size = applied.shape[0]
    applied[...] = total[pl.ds(pl.multiple_of(quarter * size, 8), size), :]


def shards(
    n, slope_matrix, prior_matrix, slope_blocks, prior_blocks,
    weight_ids, valid_mask, noise_weights, prior_weights, frames,
):
    row = lax.axis_index("row")
    col = lax.axis_index("col")
    rows, width = slope_matrix.shape
    kept = width // BS
    piece, wide = frames.shape
    classes = jnp.arange(noise_weights.shape[0], dtype=jnp.int32)
    picked = jnp.sum(
        jnp.where(weight_ids[:, None] == classes[None, :], noise_weights[None, :], 0.0), axis=1
    )
    subap_weight = picked * valid_mask.astype(jnp.float32)
    slope_weight = jnp.repeat(subap_weight, 2).astype(jnp.bfloat16)
    ids = jnp.concatenate([slope_blocks[0], prior_blocks[0]]) - col * AB
    weight = jnp.concatenate([slope_weight, prior_weights])
    extra = jnp.concatenate(
        [
            jnp.pad(ids.astype(jnp.bfloat16), (0, width - 2 * kept))[None],
            weight[None],
            jnp.zeros((EXTRA - 2, width), jnp.bfloat16),
        ]
    )
    vmem = pl.BlockSpec(memory_space=pltpu.VMEM)
    smem = pl.BlockSpec(memory_space=pltpu.SMEM)
    tall = 2 * rows + EXTRA
    pairs = pltpu.SemaphoreType.DMA((n,))
    blocks, images = pl.pallas_call(
        functools.partial(exchange, n),
        out_shape=(
            jax.ShapeDtypeStruct((2, n, tall, width), jnp.bfloat16),
            jax.ShapeDtypeStruct((n, rows, 2 * wide), jnp.bfloat16),
        ),
        in_specs=[smem] + [vmem] * 4,
        out_specs=(vmem, vmem),
        scratch_shapes=[
            pltpu.VMEM((n, tall, width), jnp.bfloat16),
            pltpu.VMEM((piece, wide), jnp.bfloat16),
            pltpu.VMEM((n * piece, wide), jnp.bfloat16),
            pltpu.VMEM((n, rows, 2 * wide), jnp.bfloat16),
            pairs, pairs, pairs, pairs, pairs, pairs,
            pltpu.SemaphoreType.DMA, pairs,
            pairs, pltpu.SemaphoreType.DMA,
            pairs, pairs, pairs, pairs,
        ],
        compiler_params=pltpu.CompilerParams(
            collective_id=0, has_side_effects=True, vmem_limit_bytes=32 * 1024 * 1024
        ),
    )(ids, slope_matrix, prior_matrix, extra, frames)
    all_ids = blocks[:, :, 2 * rows, :2 * kept].astype(jnp.float32).astype(jnp.int32).reshape(-1)
    same = jnp.where(row == col, 0, 1).astype(jnp.int32)
    all_ids = jnp.concatenate([all_ids, same[None], col[None].astype(jnp.int32)])
    gram, applied = pl.pallas_call(
        functools.partial(combine, n),
        out_shape=(
            jax.ShapeDtypeStruct((AB * BS, AB * BS), jnp.float32),
            jax.ShapeDtypeStruct((piece, wide), jnp.float32),
        ),
        in_specs=[smem, vmem, vmem],
        out_specs=(vmem, vmem),
        scratch_shapes=[pltpu.VMEM((AB * BS, wide), jnp.float32)],
        compiler_params=pltpu.CompilerParams(vmem_limit_bytes=32 * 1024 * 1024),
    )(all_ids, blocks, images)
    return gram, applied


def solution(mesh):
    in_specs = (
        P(("groups", "row"), "col"),
        P(("groups", "row"), "col"),
        P(("groups", "row"), "col"),
        P(("groups", "row"), "col"),
        P(("groups", "row")),
        P(("groups", "row")),
        P("groups"),
        P(("groups", "row")),
        P(("groups", "row", "col"), None),
    )
    out_specs = (P(("groups", "row"), "col"), P(("groups", "row", "col"), None))
    return jax.shard_map(
        functools.partial(shards, mesh.shape["row"]),
        mesh=mesh, in_specs=in_specs, out_specs=out_specs, check_vma=False,
    )
```

time: 126 us -> 41.2 us (0.33)
  waiting for transfers between devices: 54.6 us -> 0 us
  blocking collectives: 42.3 us -> 0 us
  Pallas kernels: 0 us -> 33.5 us
  between operations: 13.9 us -> 0.67 us
  matrix products: 9.43 us -> 0 us
  other arithmetic: 1.28 us -> 3.02 us
    all_gather x4 -> x0, blocking collectives: 34.6 us -> none  [the longest x1 15.8 us: shards(): frames_rows = lax.all_gather(frames, 'col', axis=0, tiled=True)]
    psum x2 -> x0, waiting for transfers between devices: 33.8 us -> none  [from_root(): return lax.psum(block, axis)]
    pallas_call x0 -> x2, Pallas kernels: none -> 33.5 us  [the longest x1 30.3 us: shards(): pl.pallas_call(functools.partial(exchange, n), out_shape=(jax.ShapeDtypeS...]
    unnamed x4 -> x0, waiting for transfers between devices: 20.8 us -> none
    psum x1 -> x0, blocking collectives: 7.77 us -> none  [from_root(): return lax.psum(block, axis)]
    dot_general x3 -> x0, matrix products: 5.77 us -> none  [the longest x2 4.3 us: expand_blocks(): jnp.einsum('rskb,rka->rsab', shaped, onehot, preferred_element_type=jnp.f...]
    unnamed x1 -> x0, matrix products: 3.66 us -> none
    unnamed x21 -> x5, local copies, waits for them, and re-layouts: 1.73 us -> 2.61 us
  transfers between devices with their start and end apart: 3 -> 0, of which waited for: 3 -> 0; matrix products, arithmetic and copies ran while one was open for 6% -> 0% of each run, Pallas kernels for 0% -> 0%
where the time goes in v1:
time: 41.2 us; the launch traced here: 41 us
  Pallas kernels  33.5 us (81%)
  local copies, waits for them, and re-layouts  3.73 us (9%)
  other arithmetic  3.02 us (7%)
  between operations  0.67 us (2%)
    pallas_call x1, Pallas kernels, shards(): pl.pallas_call(functools.partial(exchange, n), out_shape=(jax.ShapeDtypeS...  30.3 us
    pallas_call x1, Pallas kernels, shards(): pl.pallas_call(functools.partial(combine, n), out_shape=(jax.ShapeDtypeSt...  3.2 us
    unnamed x5, local copies, waits for them, and re-layouts  2.61 us

profile of v1, /device:TPU:0, one launch (start us, length us, event | category | flops | bytes accessed | tf_op | source)
XLA Modules:
  0.0 41.0 jit_solution(7345741227703015576)
XLA Ops:
  0.6 0.8 %select_reduce_fusion = f32[64]{0:T(128)S(1)} fusion(f32[16]{0:T(128)} %param.15, s32[64]{0:T(128)} %param.13), kind=kLoop, calls=%fused_computation.1 | loop fusion | flops 3008 | bytes 576 | tf_op jit(solution)/shard_map/reduce_sum | solution.py:219
  1.4 0.7 %multiply_convert_fusion = bf16[64]{0:T(256)(128)(2,1)S(1)} fusion(f32[64]{0:T(128)S(1)} %select_reduce_fusion, s32[64]{0:T(128)} %param.14), kind=kLoop, calls=%fused_computation.7 | loop fusion | flops 192 | bytes 640 | tf_op jit(solution)/shard_map/convert_element_type | solution.py:223
  2.1 0.1 pad.10.clone
  2.1 0.7 %fusion = (bf16[4]{0:T(256)(128)(2,1)S(1)}, s32[4]{0:T(128)S(1)}) fusion(s32[]{:T(128)S(6)} %mul.6, s32[2]{0:T(128)} %bitcast.4, s32[2]{0:T(128)} %bitcast.5), kind=kLoop, calls=%fused_computation.8 | loop fusion | flops 12 | bytes 44 | tf_op jit(solution)/shard_map/convert_element_type | solution.py:228
  2.9 0.1 broadcast_in_dim.36
  3.0 0.1 convert_element_type.30
  3.1 0.7 %pad_maximum_fusion = bf16[256]{0:T(256)(128)(2,1)S(1)} fusion(bf16[128]{0:T(256)(128)(2,1)} %param.16, bf16[128]{0:T(256)(128)(2,1)S(1)} %convert_element_type.30), kind=kLoop, calls=%fused_computation.5 | loop fusion | flops 1024 | bytes 1024 | tf_op jit(solution)/shard_map/concatenate | solution.py:225
  3.8 0.1 maximum_maximum_fusion.extra_ref
  3.9 0.9 %copy.15.frames_ref = f32[192,64]{1,0:T(8,128)S(1)} copy(f32[192,64]{0,1:T(8,128)} %param.17) | data formatting | bytes 98304 | tf_op args[8]
  4.8 0.0 copy-start
  4.8 0.8 %copy-done = bf16[128,256]{1,0:T(8,128)(2,1)S(1)} copy-done((bf16[128,256]{1,0:T(8,128)(2,1)S(1)}, bf16[128,256]{1,0:T(8,128)(2,1)}, u32[]{:S(2)}) %copy-start) | copy-done | bytes 65560
  5.7 0.0 copy-start.1
  5.7 0.8 %copy-done.1 = bf16[128,256]{1,0:T(8,128)(2,1)S(1)} copy-done((bf16[128,256]{1,0:T(8,128)(2,1)S(1)}, bf16[128,256]{1,0:T(8,128)(2,1)}, u32[]{:S(2)}) %copy-start.1) | copy-done | bytes 65560
  6.5 30.3 %shard_map.104 = (bf16[2,4,272,256]{3,2,1,0:T(8,128)(2,1)S(1)}, bf16[4,128,128]{2,1,0:T(8,128)(2,1)S(1)}) custom-call(s32[4]{0:T(128)S(1)} %get-tuple-element.13.ids_ref, bf16[128,256]{1,0:T(8,128)(2,1)S(1)} %copy-done, bf16[128,256]{1,0:T(8,128)(2,1)S(1)} %copy-done.1, bf16[16,256]{1,0:T(8,128)(2,1)S(1)} %maximum_maximum_fusion.extra_ref, ...), custom_call_target="tpu_custom_call" | custom-call | tf_op jit(solution)/shard_map/pallas_call | solution.py:237
  36.9 0.1 convert_element_type.33
  37.0 0.1 pad_add_fusion.ids_ref
  37.0 3.2 %shard_map.105 = (f32[768,768]{1,0:T(8,128)}, f32[192,64]{1,0:T(8,128)S(1)}) custom-call(s32[34]{0:T(128)S(1)} %pad_add_fusion.ids_ref, bf16[2,4,272,256]{3,2,1,0:T(8,128)(2,1)S(1)} %get-tuple-element.4.blocks, bf16[4,128,128]{2,1,0:T(8,128)(2,1)S(1)} %get-tuple-element.5.images), custom_call_target="tpu_custom_call" | custom-call | tf_op jit(solution)/shard_map/pallas_call | solution.py:262
  40.2 0.7 %copy.16 = f32[192,64]{0,1:T(8,128)} copy(f32[192,64]{1,0:T(8,128)S(1)} %get-tuple-element.11) | data formatting | bytes 98304 | tf_op jit(solution)/shard_map/pallas_call | solution.py:262
  (5 shorter events, 0.0 us)
Async XLA Ops:
  4.8 0.8 %copy-start = (bf16[128,256]{1,0:T(8,128)(2,1)S(1)}, bf16[128,256]{1,0:T(8,128)(2,1)}, u32[]{:S(2)}) copy-start(bf16[128,256]{1,0:T(8,128)(2,1)} %slope_ref.1) | copy-start | bytes 196612
  5.7 0.8 %copy-start.1 = (bf16[128,256]{1,0:T(8,128)(2,1)S(1)}, bf16[128,256]{1,0:T(8,128)(2,1)}, u32[]{:S(2)}) copy-start(bf16[128,256]{1,0:T(8,128)(2,1)} %prior_ref.1) | copy-start | bytes 196612

commit v2 on v1

--- a/solution.py
+++ b/solution.py
@@ -21,24 +21,63 @@
 
 
 def exchange(
-    n, ids_ref, slope_ref, prior_ref, extra_ref, frames_ref,
+    n, classes, slope_hbm, prior_hbm, slope_ids_hbm, prior_ids_hbm,
+    class_hbm, valid_hbm, noise_hbm, prior_weight_hbm, frames_hbm,
     blocks, images,
     held, own_frames, set_frames, partial,
-    send_z, recv_z, send_c, recv_c, send_r, recv_r,
+    slope_ids, prior_ids, class_ids, valid, noise, prior_weight, frames_ref, load_sem,
+    send_right, send_left, recv_z, send_c, recv_c, send_r, recv_r,
     send_p, recv_p, send_f, recv_f, send_v, recv_v, send_u, recv_u,
 ):
     row = lax.axis_index("row")
     col = lax.axis_index("col")
-    rows = slope_ref.shape[0]
+    rows, width = slope_hbm.shape
+    kept = width // BS
     piece = own_frames.shape[0]
+    loads = [
+        pltpu.make_async_copy(src, dst, load_sem.at[k])
+        for k, (src, dst) in enumerate(
+            (
+                (class_hbm, class_ids), (valid_hbm, valid), (noise_hbm, noise),
+                (prior_weight_hbm, prior_weight), (slope_ids_hbm, slope_ids),
+                (prior_ids_hbm, prior_ids), (frames_hbm, frames_ref),
+                (slope_hbm, held.at[col, pl.ds(0, rows), :]),
+                (prior_hbm, held.at[col, pl.ds(rows, rows), :]),
+            )
+        )
+    ]
+    for load in loads:
+        load.start()
     barrier = pltpu.get_barrier_semaphore()
     for t in range(1, n):
         pl.semaphore_signal(barrier, inc=1, device_id={"col": lax.rem(col + t, n)}, device_id_type=MESH)
         pl.semaphore_signal(barrier, inc=1, device_id={"row": lax.rem(row + t, n)}, device_id_type=MESH)
-    own_frames[...] = frames_ref[...].astype(jnp.bfloat16)
-    held[col, pl.ds(0, rows), :] = slope_ref[...]
-    held[col, pl.ds(rows, rows), :] = prior_ref[...]
-    held[col, pl.ds(2 * rows, EXTRA), :] = extra_ref[...]
+    for load in loads:
+        load.wait()
+    own_frames[...] = jnp.transpose(frames_ref[...]).astype(jnp.bfloat16)
+    subaps = class_ids.shape[1]
+    picked = jnp.zeros((1, subaps), jnp.float32)
+    for k in range(classes):
+        picked = jnp.where(class_ids[...] == k, jnp.broadcast_to(noise[:, k:k + 1], picked.shape), picked)
+    picked = (picked * valid[...].astype(jnp.float32)).astype(jnp.bfloat16)
+    first = lax.broadcasted_iota(jnp.int32, (subaps, rows), 0) * (rows // subaps)
+    lane = lax.broadcasted_iota(jnp.int32, (subaps, rows), 1)
+    spread = (lane >= first) & (lane < first + rows // subaps)
+    spread = jnp.where(spread, 1.0, 0.0).astype(jnp.bfloat16)
+    slope_weight = jnp.dot(
+        jnp.broadcast_to(picked, (EXTRA, subaps)), spread, preferred_element_type=jnp.float32
+    )
+    prior_wide = jnp.broadcast_to(prior_weight[...].astype(jnp.float32), (EXTRA, rows))
+    weight = jnp.concatenate([slope_weight, prior_wide], axis=1)
+    at_row = lax.broadcasted_iota(jnp.int32, (EXTRA, width), 0)
+    at_lane = lax.broadcasted_iota(jnp.int32, (EXTRA, width), 1)
+    names = jnp.zeros((EXTRA, width), jnp.int32)
+    for part, ids in enumerate((slope_ids, prior_ids)):
+        for k in range(kept):
+            name = jnp.broadcast_to(ids[:, k:k + 1], names.shape) - col * AB
+            names = jnp.where(at_lane == part * kept + k, name, names)
+    extra = jnp.where(at_row == 0, names.astype(jnp.float32), weight)
+    held[col, pl.ds(2 * rows, EXTRA), :] = extra.astype(jnp.bfloat16)
     pl.semaphore_wait(barrier, 2 * (n - 1))
 
     def frame_piece(source):
@@ -47,34 +86,68 @@
             send_p, recv_p.at[source], "col", row,
         )
 
+    def right(t):
+        source = col - t
+        return remote(
+            held.at[source], held.at[source], send_right.at[t], recv_z.at[source], "col", col + 1
+        )
+
+    def left(t):
+        source = col + t
+        return remote(
+            held.at[source], held.at[source], send_left.at[t], recv_z.at[source], "col", col - 1
+        )
+
+    sibling = row + 1 - 2 * lax.rem(row, 2)
+
+    def own_column(m):
+        to = sibling if m == 0 else lax.rem(row + 2 * m, n)
+        return remote(held.at[col], blocks.at[0, row], send_c.at[m], recv_c.at[row], "row", to)
+
+    def pass_column(m):
+        source = lax.rem(row + 2 * m, n)
+        return remote(
+            blocks.at[0, source], blocks.at[0, source], send_c.at[n // 2 + m], recv_c.at[source], "row", sibling
+        )
+
+    def came_column(source):
+        return remote(blocks.at[0, source], blocks.at[0, source], send_c.at[0], recv_c.at[source], "row", sibling)
+
+    def forward(source):
+        return remote(
+            held.at[source], blocks.at[1, row], send_r.at[source], recv_r.at[row], "row", source
+        )
+
+    def came_row(source):
+        return remote(
+            held.at[source], blocks.at[1, source], send_r.at[source], recv_r.at[source], "row", source
+        )
+
+    def whole_frames(s):
+        return remote(
+            set_frames, set_frames, send_f.at[s - 1], recv_f, "row", lax.rem(row + s, n)
+        )
+
     @pl.when(row != col)
     def _():
         frame_piece(col).start()
 
-    sends_z = []
-    for t in range(1, n):
-        copy = remote(
-            held.at[col], held.at[col], send_z.at[t - 1], recv_z.at[t - 1], "col", lax.rem(col + t, n)
-        )
-        copy.start()
-        sends_z.append(copy)
-    sends_c = []
-    for s in range(1, n):
-        copy = remote(
-            held.at[col], blocks.at[0, row], send_c.at[s - 1], recv_c.at[s - 1], "row", lax.rem(row + s, n)
-        )
-        copy.start()
-        sends_c.append(copy)
+    @pl.when(col < n - 1)
+    def _():
+        right(0).start()
+
+    @pl.when(col > 0)
+    def _():
+        left(0).start()
+
+    for m in range(1, n // 2):
+        own_column(m).start()
+    own_column(0).start()
     blocks[0, row] = held[col]
 
-    def whole_frames(s):
-        return remote(
-            set_frames, set_frames, send_f.at[s - 1], recv_f, "row", lax.rem(row + s, n)
-        )
-
     @pl.when(row == col)
     def _():
-        set_frames[pl.ds(col * piece, piece), :] = own_frames[...]
+        set_frames[pl.ds(pl.multiple_of(col * piece, 16), piece), :] = own_frames[...]
         for t in range(1, n):
             frame_piece(lax.rem(col + t, n)).wait_recv()
         for s in range(1, n):
@@ -85,16 +158,16 @@
         whole_frames(1).wait_recv()
 
     parts = []
-    for part, ref in enumerate((slope_ref, prior_ref)):
+    for part, ids in enumerate((slope_ids, prior_ids)):
         total = jnp.zeros((rows, set_frames.shape[1]), jnp.float32)
-        for k in range(ref.shape[1] // BS):
-            wanted = jnp.full((BS, set_frames.shape[1]), ids_ref[part * (ref.shape[1] // BS) + k], jnp.int32)
+        for k in range(kept):
+            wanted = jnp.broadcast_to(ids[:, k:k + 1], (BS, set_frames.shape[1])) - col * AB
             chosen = jnp.zeros(wanted.shape, jnp.float32)
             for a in range(AB):
                 block = set_frames[a * BS:(a + 1) * BS, :].astype(jnp.float32)
                 chosen = jnp.where(wanted == a, block, chosen)
             total += jnp.dot(
-                ref[:, k * BS:(k + 1) * BS], chosen.astype(jnp.bfloat16),
+                held[col, part * rows:(part + 1) * rows, k * BS:(k + 1) * BS], chosen.astype(jnp.bfloat16),
                 preferred_element_type=jnp.float32,
             )
         parts.append(total)
@@ -107,24 +180,41 @@
         copy.start()
         sends_v.append(copy)
 
-    def forward(t):
-        source = lax.rem(col + n - t, n)
-        return remote(
-            held.at[source], blocks.at[1, row], send_r.at[t - 1],
-            recv_r.at[lax.rem(source + n - row, n)], "row", source,
-        )
-
-    for t in range(1, n):
-        sends_z[t - 1].wait_recv()
-        source = lax.rem(col + n - t, n)
-
+    def use(source):
         @pl.when(source == row)
         def _():
             blocks[1, row] = held[row]
 
         @pl.when(source != row)
         def _():
-            forward(t).start()
+            forward(source).start()
+
+    for t in range(1, n):
+        @pl.when(col - t >= 0)
+        def _():
+            came = right(t)
+            came.wait_recv()
+
+            @pl.when(col < n - 1)
+            def _():
+                came.start()
+
+            use(col - t)
+
+        @pl.when(col + t < n)
+        def _():
+            came = left(t)
+            came.wait_recv()
+
+            @pl.when(col > 0)
+            def _():
+                came.start()
+
+            use(col + t)
+
+        if t < n // 2:
+            came_column(lax.rem(row + 2 * t, n)).wait_recv()
+            pass_column(t).start()
 
     for copy in sends_v:
         copy.wait_recv()
@@ -140,16 +230,13 @@
         copy.start()
         sends_u.append(copy)
 
-    for copy in sends_c:
-        copy.wait_recv()
+    for m in range(n // 2):
+        came_column(lax.rem(sibling + 2 * m, n)).wait_recv()
 
     @pl.when(row != col)
     def _():
         for s in range(1, n):
-            source = lax.rem(row + n - s, n)
-            remote(
-                held.at[0], blocks.at[1, source], send_r.at[0], recv_r.at[s], "row", source
-            ).wait_recv()
+            came_row(lax.rem(row + s, n)).wait_recv()
         frame_piece(col).wait_send()
 
     @pl.when(row == col)
@@ -160,12 +247,26 @@
     for copy in sends_u:
         copy.wait_recv()
     for t in range(1, n):
-
-        @pl.when(lax.rem(col + n - t, n) != row)
-        def _():
-            forward(t).wait_send()
-
-    for copy in sends_z + sends_c + sends_v + sends_u:
+        source = lax.rem(col + t, n)
+
+        @pl.when(source != row)
+        def _():
+            forward(source).wait_send()
+
+    for t in range(n):
+        @pl.when((col - t >= 0) & (col < n - 1))
+        def _():
+            right(t).wait_send()
+
+        @pl.when((col + t < n) & (col > 0))
+        def _():
+            left(t).wait_send()
+
+    for m in range(n // 2):
+        own_column(m).wait_send()
+        if m > 0:
+            pass_column(m).wait_send()
+    for copy in sends_v + sends_u:
         copy.wait_send()
 
 
@@ -202,8 +303,8 @@
                     gram[pl.ds(down, BS), pl.ds(across, BS)] += product[
                         a * BS:(a + 1) * BS, b * BS:(b + 1) * BS
                     ]
-    size = applied.shape[0]
-    applied[...] = total[pl.ds(pl.multiple_of(quarter * size, 8), size), :]
+    size = applied.shape[1]
+    applied[...] = jnp.transpose(total[pl.ds(pl.multiple_of(quarter * size, 8), size), :])
 
 
 def shards(
@@ -215,39 +316,32 @@
     rows, width = slope_matrix.shape
     kept = width // BS
     piece, wide = frames.shape
-    classes = jnp.arange(noise_weights.shape[0], dtype=jnp.int32)
-    picked = jnp.sum(
-        jnp.where(weight_ids[:, None] == classes[None, :], noise_weights[None, :], 0.0), axis=1
-    )
-    subap_weight = picked * valid_mask.astype(jnp.float32)
-    slope_weight = jnp.repeat(subap_weight, 2).astype(jnp.bfloat16)
-    ids = jnp.concatenate([slope_blocks[0], prior_blocks[0]]) - col * AB
-    weight = jnp.concatenate([slope_weight, prior_weights])
-    extra = jnp.concatenate(
-        [
-            jnp.pad(ids.astype(jnp.bfloat16), (0, width - 2 * kept))[None],
-            weight[None],
-            jnp.zeros((EXTRA - 2, width), jnp.bfloat16),
-        ]
-    )
     vmem = pl.BlockSpec(memory_space=pltpu.VMEM)
     smem = pl.BlockSpec(memory_space=pltpu.SMEM)
     tall = 2 * rows + EXTRA
     pairs = pltpu.SemaphoreType.DMA((n,))
+    small = (
+        slope_blocks, prior_blocks, weight_ids[None], valid_mask[None],
+        noise_weights[None], prior_weights[None], frames.T,
+    )
     blocks, images = pl.pallas_call(
-        functools.partial(exchange, n),
+        functools.partial(exchange, n, noise_weights.shape[0]),
         out_shape=(
             jax.ShapeDtypeStruct((2, n, tall, width), jnp.bfloat16),
             jax.ShapeDtypeStruct((n, rows, 2 * wide), jnp.bfloat16),
         ),
-        in_specs=[smem] + [vmem] * 4,
+        in_specs=[pl.BlockSpec(memory_space=pltpu.HBM)] * 9,
         out_specs=(vmem, vmem),
         scratch_shapes=[
             pltpu.VMEM((n, tall, width), jnp.bfloat16),
             pltpu.VMEM((piece, wide), jnp.bfloat16),
             pltpu.VMEM((n * piece, wide), jnp.bfloat16),
             pltpu.VMEM((n, rows, 2 * wide), jnp.bfloat16),
-            pairs, pairs, pairs, pairs, pairs, pairs,
+        ]
+        + [pltpu.VMEM(x.shape, x.dtype) for x in small]
+        + [
+            pltpu.SemaphoreType.DMA((9,)),
+            pairs, pairs, pairs, pairs, pairs, pairs, pairs,
             pltpu.SemaphoreType.DMA, pairs,
             pairs, pltpu.SemaphoreType.DMA,
             pairs, pairs, pairs, pairs,
@@ -255,7 +349,10 @@
         compiler_params=pltpu.CompilerParams(
             collective_id=0, has_side_effects=True, vmem_limit_bytes=32 * 1024 * 1024
         ),
-    )(ids, slope_matrix, prior_matrix, extra, frames)
+    )(
+        slope_matrix, prior_matrix, slope_blocks, prior_blocks, weight_ids[None], valid_mask[None],
+        noise_weights[None], prior_weights[None], frames.T,
+    )
     all_ids = blocks[:, :, 2 * rows, :2 * kept].astype(jnp.float32).astype(jnp.int32).reshape(-1)
     same = jnp.where(row == col, 0, 1).astype(jnp.int32)
     all_ids = jnp.concatenate([all_ids, same[None], col[None].astype(jnp.int32)])
@@ -263,14 +360,14 @@
         functools.partial(combine, n),
         out_shape=(
             jax.ShapeDtypeStruct((AB * BS, AB * BS), jnp.float32),
-            jax.ShapeDtypeStruct((piece, wide), jnp.float32),
+            jax.ShapeDtypeStruct((wide, piece), jnp.float32),
         ),
         in_specs=[smem, vmem, vmem],
         out_specs=(vmem, vmem),
         scratch_shapes=[pltpu.VMEM((AB * BS, wide), jnp.float32)],
         compiler_params=pltpu.CompilerParams(vmem_limit_bytes=32 * 1024 * 1024),
     )(all_ids, blocks, images)
-    return gram, applied
+    return gram, applied.T
 
 
 def solution(mesh):

time: 41.2 us -> 42.2 us (1.024)
  other arithmetic: 3.02 us -> 0.1 us
  local copies, waits for them, and re-layouts: 3.73 us -> 6.52 us
  Pallas kernels: 33.5 us -> 34.6 us
    unnamed x5 -> x18, local copies, waits for them, and re-layouts: 2.61 us -> 6.44 us
    convert_element_type x2 -> x0, other arithmetic: 1.41 us -> none  [the longest x1 0.75 us: shards(): ids.astype(jnp.bfloat16)]
    pallas_call x1, Pallas kernels: 30.3 us -> 31.4 us  [shards(): pl.pallas_call(functools.partial(exchange, n, noise_weights.shape[0]), ou...]
    reduce_sum x1 -> x0, other arithmetic: 0.76 us -> none  [shards(): jnp.sum(jnp.where(weight_ids[:, None] == classes[None, :], noise_weights[...]
    concatenate x2 -> x0, other arithmetic: 0.74 us -> none  [the longest x1 0.67 us: shards(): weight = jnp.concatenate([slope_weight, prior_weights])]
    pallas_call x1 -> x0, local copies, waits for them, and re-layouts: 0.71 us -> none  [shards(): pl.pallas_call(functools.partial(combine, n), out_shape=(jax.ShapeDtypeSt...]
where the time goes in v2:
time: 42.2 us; the launch traced here: 41.9 us
  Pallas kernels  34.6 us (82%)
  local copies, waits for them, and re-layouts  6.52 us (15%)
  between operations  0.67 us (2%)
    pallas_call x1, Pallas kernels, shards(): pl.pallas_call(functools.partial(exchange, n, noise_weights.shape[0]), ou...  31.4 us
    unnamed x18, local copies, waits for them, and re-layouts  6.44 us
    pallas_call x1, Pallas kernels, shards(): pl.pallas_call(functools.partial(combine, n), out_shape=(jax.ShapeDtypeSt...  3.19 us

profile of v2, /device:TPU:0, one launch (start us, length us, event | category | flops | bytes accessed | tf_op | source)
XLA Modules:
  0.0 41.9 jit_solution(14360755140684663233)
XLA Ops:
  0.6 0.0 copy-start
  0.7 0.8 %copy-done = bf16[128,256]{1,0:T(8,128)(2,1)S(1)} copy-done((bf16[128,256]{1,0:T(8,128)(2,1)S(1)}, bf16[128,256]{1,0:T(8,128)(2,1)}, u32[]{:S(2)}) %copy-start) | copy-done | bytes 65560
  1.5 0.0 copy-start.1
  1.5 0.8 %copy-done.1 = bf16[128,256]{1,0:T(8,128)(2,1)S(1)} copy-done((bf16[128,256]{1,0:T(8,128)(2,1)S(1)}, bf16[128,256]{1,0:T(8,128)(2,1)}, u32[]{:S(2)}) %copy-start.1) | copy-done | bytes 65560
  2.3 0.0 copy-start.2
  2.3 0.8 %copy-done.2 = f32[192,64]{0,1:T(8,128)S(1)} copy-done((f32[192,64]{0,1:T(8,128)S(1)}, f32[192,64]{0,1:T(8,128)}, u32[]{:S(2)}) %copy-start.2) | copy-done | bytes 49176
  3.2 0.0 copy-start.3
  3.2 0.7 %copy-done.3 = s32[1,2]{1,0:T(1,128)S(1)} copy-done((s32[1,2]{1,0:T(1,128)S(1)}, s32[1,2]{1,0:T(1,128)}, u32[]{:S(2)}) %copy-start.3) | copy-done | bytes 32
  3.8 0.0 copy-start.4
  3.8 0.7 %copy-done.4 = s32[1,2]{1,0:T(1,128)S(1)} copy-done((s32[1,2]{1,0:T(1,128)S(1)}, s32[1,2]{1,0:T(1,128)}, u32[]{:S(2)}) %copy-start.4) | copy-done | bytes 32
  4.5 0.0 copy-start.5
  4.5 0.7 %copy-done.5 = s32[64]{0:T(128)S(1)} copy-done((s32[64]{0:T(128)S(1)}, s32[64]{0:T(128)}, u32[]{:S(2)}) %copy-start.5) | copy-done | bytes 280
  5.1 0.0 copy-start.6
  5.1 0.7 %copy-done.6 = s32[64]{0:T(128)S(1)} copy-done((s32[64]{0:T(128)S(1)}, s32[64]{0:T(128)}, u32[]{:S(2)}) %copy-start.6) | copy-done | bytes 280
  5.8 0.0 copy-start.7
  5.8 0.7 %copy-done.7 = f32[16]{0:T(128)S(1)} copy-done((f32[16]{0:T(128)S(1)}, f32[16]{0:T(128)}, u32[]{:S(2)}) %copy-start.7) | copy-done | bytes 88
  6.4 0.0 copy-start.8
  6.4 0.7 %copy-done.8 = bf16[128]{0:T(256)(128)(2,1)S(1)} copy-done((bf16[128]{0:T(256)(128)(2,1)S(1)}, bf16[128]{0:T(256)(128)(2,1)}, u32[]{:S(2)}) %copy-start.8) | copy-done | bytes 280
  7.1 31.4 %shard_map.104 = (bf16[2,4,272,256]{3,2,1,0:T(8,128)(2,1)S(1)}, bf16[4,128,128]{2,1,0:T(8,128)(2,1)S(1)}) custom-call(bf16[128,256]{1,0:T(8,128)(2,1)S(1)} %copy-done, bf16[128,256]{1,0:T(8,128)(2,1)S(1)} %copy-done.1, s32[1,2]{1,0:T(1,128)S(1)} %copy-done.3, s32[1,2]{1,0:T(1,128)S(1)} %copy-done.4, s32[1,64]{1,0:T(1,128)S(1)} %bitcast.9, ...), custom_call_target="tpu_custom_call" | custom-call | tf_op jit(solution)/shard_map/pallas_call | solution.py:327
  38.5 0.1 convert_element_type.14
  38.6 0.1 pad_add_fusion.ids_ref
  38.7 3.2 %shard_map.105 = (f32[768,768]{1,0:T(8,128)}, f32[64,192]{1,0:T(8,128)}) custom-call(s32[34]{0:T(128)S(1)} %pad_add_fusion.ids_ref, bf16[2,4,272,256]{3,2,1,0:T(8,128)(2,1)S(1)} %get-tuple-element.6.blocks, bf16[4,128,128]{2,1,0:T(8,128)(2,1)S(1)} %get-tuple-element.7.images), custom_call_target="tpu_custom_call" | custom-call | tf_op jit(solution)/shard_map/pallas_call | solution.py:359
  (1 shorter events, 0.0 us)
Async XLA Ops:
  0.6 0.8 %copy-start = (bf16[128,256]{1,0:T(8,128)(2,1)S(1)}, bf16[128,256]{1,0:T(8,128)(2,1)}, u32[]{:S(2)}) copy-start(bf16[128,256]{1,0:T(8,128)(2,1)} %slope_hbm.1) | copy-start | bytes 196612
  1.5 0.8 %copy-start.1 = (bf16[128,256]{1,0:T(8,128)(2,1)S(1)}, bf16[128,256]{1,0:T(8,128)(2,1)}, u32[]{:S(2)}) copy-start(bf16[128,256]{1,0:T(8,128)(2,1)} %prior_hbm.1) | copy-start | bytes 196612
  2.3 0.8 %copy-start.2 = (f32[192,64]{0,1:T(8,128)S(1)}, f32[192,64]{0,1:T(8,128)}, u32[]{:S(2)}) copy-start(f32[192,64]{0,1:T(8,128)} %param.17) | copy-start | bytes 147460
  3.2 0.7 %copy-start.3 = (s32[1,2]{1,0:T(1,128)S(1)}, s32[1,2]{1,0:T(1,128)}, u32[]{:S(2)}) copy-start(s32[1,2]{1,0:T(1,128)} %slope_ids_hbm.1) | copy-start | bytes 28
  3.8 0.7 %copy-start.4 = (s32[1,2]{1,0:T(1,128)S(1)}, s32[1,2]{1,0:T(1,128)}, u32[]{:S(2)}) copy-start(s32[1,2]{1,0:T(1,128)} %prior_ids_hbm.1) | copy-start | bytes 28
  4.5 0.7 %copy-start.5 = (s32[64]{0:T(128)S(1)}, s32[64]{0:T(128)}, u32[]{:S(2)}) copy-start(s32[64]{0:T(128)} %param.13) | copy-start | bytes 772
  5.1 0.7 %copy-start.6 = (s32[64]{0:T(128)S(1)}, s32[64]{0:T(128)}, u32[]{:S(2)}) copy-start(s32[64]{0:T(128)} %param.14) | copy-start | bytes 772
  5.8 0.7 %copy-start.7 = (f32[16]{0:T(128)S(1)}, f32[16]{0:T(128)}, u32[]{:S(2)}) copy-start(f32[16]{0:T(128)} %param.15) | copy-start | bytes 196
  6.4 0.7 %copy-start.8 = (bf16[128]{0:T(256)(128)(2,1)S(1)}, bf16[128]{0:T(256)(128)(2,1)}, u32[]{:S(2)}) copy-start(bf16[128]{0:T(256)(128)(2,1)} %param.16) | copy-start | bytes 772

commit v3 on v2

--- a/solution.py
+++ b/solution.py
@@ -140,11 +140,6 @@
     def _():
         left(0).start()
 
-    for m in range(1, n // 2):
-        own_column(m).start()
-    own_column(0).start()
-    blocks[0, row] = held[col]
-
     @pl.when(row == col)
     def _():
         set_frames[pl.ds(pl.multiple_of(col * piece, 16), piece), :] = own_frames[...]
@@ -152,6 +147,49 @@
             frame_piece(lax.rem(col + t, n)).wait_recv()
         for s in range(1, n):
             whole_frames(s).start()
+
+    for m in range(1, n // 2):
+        own_column(m).start()
+    own_column(0).start()
+    blocks[0, row] = held[col]
+
+    def use(source):
+        @pl.when(source == row)
+        def _():
+            blocks[1, row] = held[row]
+
+        @pl.when(source != row)
+        def _():
+            forward(source).start()
+
+    def step(t):
+        @pl.when(col - t >= 0)
+        def _():
+            came = right(t)
+            came.wait_recv()
+
+            @pl.when(col < n - 1)
+            def _():
+                came.start()
+
+            use(col - t)
+
+        @pl.when(col + t < n)
+        def _():
+            came = left(t)
+            came.wait_recv()
+
+            @pl.when(col > 0)
+            def _():
+                came.start()
+
+            use(col + t)
+
+        if t < n // 2:
+            came_column(lax.rem(row + 2 * t, n)).wait_recv()
+            pass_column(t).start()
+
+    step(1)
 
     @pl.when(row != col)
     def _():
@@ -180,41 +218,8 @@
         copy.start()
         sends_v.append(copy)
 
-    def use(source):
-        @pl.when(source == row)
-        def _():
-            blocks[1, row] = held[row]
-
-        @pl.when(source != row)
-        def _():
-            forward(source).start()
-
-    for t in range(1, n):
-        @pl.when(col - t >= 0)
-        def _():
-            came = right(t)
-            came.wait_recv()
-
-            @pl.when(col < n - 1)
-            def _():
-                came.start()
-
-            use(col - t)
-
-        @pl.when(col + t < n)
-        def _():
-            came = left(t)
-            came.wait_recv()
-
-            @pl.when(col > 0)
-            def _():
-                came.start()
-
-            use(col + t)
-
-        if t < n // 2:
-            came_column(lax.rem(row + 2 * t, n)).wait_recv()
-            pass_column(t).start()
+    for t in range(2, n):
+        step(t)
 
     for copy in sends_v:
         copy.wait_recv()
@@ -347,7 +352,7 @@
             pairs, pairs, pairs, pairs,
         ],
         compiler_params=pltpu.CompilerParams(
-            collective_id=0, has_side_effects=True, vmem_limit_bytes=32 * 1024 * 1024
+            collective_id=0, has_side_effects=True, vmem_limit_bytes=62 * 1024 * 1024
         ),
     )(
         slope_matrix, prior_matrix, slope_blocks, prior_blocks, weight_ids[None], valid_mask[None],

time: 42.2 us -> 35.3 us (0.84)
  local copies, waits for them, and re-layouts: 6.52 us -> 2.24 us
  Pallas kernels: 34.6 us -> 31.3 us
  other arithmetic: 0.1 us -> 0.82 us
    unnamed x18 -> x4, local copies, waits for them, and re-layouts: 6.44 us -> 2.16 us
    pallas_call x1, Pallas kernels: 31.4 us -> 28.1 us  [shards(): pl.pallas_call(functools.partial(exchange, n, noise_weights.shape[0]), ou...]
    convert_element_type x1, other arithmetic: 0.03 us -> 0.74 us  [shards(): blocks[:, :, 2 * rows, :2 * kept].astype(jnp.float32).astype(jnp.int32)]
where the time goes in v3:
time: 35.3 us; the launch traced here: 35 us
  Pallas kernels  31.3 us (89%)
  local copies, waits for them, and re-layouts  2.24 us (6%)
  other arithmetic  0.82 us (2%)
  between operations  0.65 us (2%)
    pallas_call x1, Pallas kernels, shards(): pl.pallas_call(functools.partial(exchange, n, noise_weights.shape[0]), ou...  28.1 us
    pallas_call x1, Pallas kernels, shards(): pl.pallas_call(functools.partial(combine, n), out_shape=(jax.ShapeDtypeSt...  3.19 us
    unnamed x4, local copies, waits for them, and re-layouts  2.16 us
    convert_element_type x1, other arithmetic, shards(): blocks[:, :, 2 * rows, :2 * kept].astype(jnp.float32).astype(jnp.int32)  0.74 us

profile of v3, /device:TPU:0, one launch (start us, length us, event | category | flops | bytes accessed | tf_op | source)
XLA Modules:
  0.0 35.0 jit_solution(4273295597524184378)
XLA Ops:
  0.6 28.1 %shard_map.104 = (bf16[2,4,272,256]{3,2,1,0:T(8,128)(2,1)}, bf16[4,128,128]{2,1,0:T(8,128)(2,1)}) custom-call(bf16[128,256]{1,0:T(8,128)(2,1)} %slope_hbm.1, bf16[128,256]{1,0:T(8,128)(2,1)} %prior_hbm.1, s32[1,2]{1,0:T(1,128)} %slope_ids_hbm.1, s32[1,2]{1,0:T(1,128)} %prior_ids_hbm.1, s32[1,64]{1,0:T(1,128)} %bitcast.9, s32[1,64]{1,0:T(1,128)} %bitcast.10, ...), custom_call_target="tpu_custom_call" | custom-call | tf_op jit(solution)/shard_map/pallas_call | solution.py:332
  28.8 0.7 %convert_reduce_fusion = s32[2,4,4]{2,1,0:T(4,128)S(1)} fusion(bf16[2,4,272,256]{3,2,1,0:T(8,128)(2,1)} %get-tuple-element.6.blocks), kind=kLoop, calls=%fused_computation | loop fusion | flops 64 | bytes 192 | tf_op jit(solution)/shard_map/convert_element_type | solution.py:361
  29.5 0.1 convert_element_type.14
  29.6 0.1 pad_add_fusion.ids_ref
  29.7 0.0 copy-start
  29.7 1.3 %copy-done = bf16[2,4,272,256]{3,2,1,0:T(8,128)(2,1)S(1)} copy-done((bf16[2,4,272,256]{3,2,1,0:T(8,128)(2,1)S(1)}, bf16[2,4,272,256]{3,2,1,0:T(8,128)(2,1)}, u32[]{:S(2)}) %copy-start) | copy-done | bytes 1114136
  30.9 0.0 copy-start.1
  30.9 0.9 %copy-done.1 = bf16[4,128,128]{2,1,0:T(8,128)(2,1)S(1)} copy-done((bf16[4,128,128]{2,1,0:T(8,128)(2,1)S(1)}, bf16[4,128,128]{2,1,0:T(8,128)(2,1)}, u32[]{:S(2)}) %copy-start.1) | copy-done | bytes 131096
  31.8 3.2 %shard_map.105 = (f32[768,768]{1,0:T(8,128)}, f32[64,192]{1,0:T(8,128)}) custom-call(s32[34]{0:T(128)S(1)} %pad_add_fusion.ids_ref, bf16[2,4,272,256]{3,2,1,0:T(8,128)(2,1)S(1)} %copy-done, bf16[4,128,128]{2,1,0:T(8,128)(2,1)S(1)} %copy-done.1), custom_call_target="tpu_custom_call" | custom-call | tf_op jit(solution)/shard_map/pallas_call | solution.py:364
Async XLA Ops:
  29.7 1.3 %copy-start = (bf16[2,4,272,256]{3,2,1,0:T(8,128)(2,1)S(1)}, bf16[2,4,272,256]{3,2,1,0:T(8,128)(2,1)}, u32[]{:S(2)}) copy-start(bf16[2,4,272,256]{3,2,1,0:T(8,128)(2,1)} %get-tuple-element.6.blocks) | copy-start | bytes 3342340
  30.9 0.9 %copy-start.1 = (bf16[4,128,128]{2,1,0:T(8,128)(2,1)S(1)}, bf16[4,128,128]{2,1,0:T(8,128)(2,1)}, u32[]{:S(2)}) copy-start(bf16[4,128,128]{2,1,0:T(8,128)(2,1)} %get-tuple-element.7.images) | copy-start | bytes 393220

commit v4 on v3

--- a/solution.py
+++ b/solution.py
@@ -24,7 +24,7 @@
     n, classes, slope_hbm, prior_hbm, slope_ids_hbm, prior_ids_hbm,
     class_hbm, valid_hbm, noise_hbm, prior_weight_hbm, frames_hbm,
     blocks, images,
-    held, own_frames, set_frames, partial,
+    held, own_frames, set_frames, flat_frames, partial,
     slope_ids, prior_ids, class_ids, valid, noise, prior_weight, frames_ref, load_sem,
     send_right, send_left, recv_z, send_c, recv_c, send_r, recv_r,
     send_p, recv_p, send_f, recv_f, send_v, recv_v, send_u, recv_u,
@@ -54,7 +54,11 @@
         pl.semaphore_signal(barrier, inc=1, device_id={"row": lax.rem(row + t, n)}, device_id_type=MESH)
     for load in loads:
         load.wait()
-    own_frames[...] = jnp.transpose(frames_ref[...]).astype(jnp.bfloat16)
+    turned = jnp.transpose(frames_ref[...])
+    pack = turned.shape[0] // piece
+    own_frames[...] = jnp.concatenate(
+        [turned[h * piece:(h + 1) * piece] for h in range(pack)], axis=1
+    ).astype(jnp.bfloat16)
     subaps = class_ids.shape[1]
     picked = jnp.zeros((1, subaps), jnp.float32)
     for k in range(classes):
@@ -195,14 +199,20 @@
     def _():
         whole_frames(1).wait_recv()
 
+    wide = turned.shape[1]
+    for k in range(n):
+        for h in range(pack):
+            flat_frames[pl.ds((k * pack + h) * piece, piece), :] = set_frames[
+                k * piece:(k + 1) * piece, h * wide:(h + 1) * wide
+            ]
     parts = []
     for part, ids in enumerate((slope_ids, prior_ids)):
-        total = jnp.zeros((rows, set_frames.shape[1]), jnp.float32)
+        total = jnp.zeros((rows, wide), jnp.float32)
         for k in range(kept):
-            wanted = jnp.broadcast_to(ids[:, k:k + 1], (BS, set_frames.shape[1])) - col * AB
+            wanted = jnp.broadcast_to(ids[:, k:k + 1], (BS, wide)) - col * AB
             chosen = jnp.zeros(wanted.shape, jnp.float32)
             for a in range(AB):
-                block = set_frames[a * BS:(a + 1) * BS, :].astype(jnp.float32)
+                block = flat_frames[a * BS:(a + 1) * BS, :].astype(jnp.float32)
                 chosen = jnp.where(wanted == a, block, chosen)
             total += jnp.dot(
                 held[col, part * rows:(part + 1) * rows, k * BS:(k + 1) * BS], chosen.astype(jnp.bfloat16),
@@ -218,7 +228,7 @@
         copy.start()
         sends_v.append(copy)
 
-    for t in range(2, n):
+    for t in range(2, n - 1):
         step(t)
 
     for copy in sends_v:
@@ -234,6 +244,8 @@
         )
         copy.start()
         sends_u.append(copy)
+
+    step(n - 1)
 
     for m in range(n // 2):
         came_column(lax.rem(sibling + 2 * m, n)).wait_recv()
@@ -324,6 +336,7 @@
     vmem = pl.BlockSpec(memory_space=pltpu.VMEM)
     smem = pl.BlockSpec(memory_space=pltpu.SMEM)
     tall = 2 * rows + EXTRA
+    pack = 2 if piece % 32 == 0 else 1
     pairs = pltpu.SemaphoreType.DMA((n,))
     small = (
         slope_blocks, prior_blocks, weight_ids[None], valid_mask[None],
@@ -339,7 +352,8 @@
         out_specs=(vmem, vmem),
         scratch_shapes=[
             pltpu.VMEM((n, tall, width), jnp.bfloat16),
-            pltpu.VMEM((piece, wide), jnp.bfloat16),
+            pltpu.VMEM((piece // pack, wide * pack), jnp.bfloat16),
+            pltpu.VMEM((n * piece // pack, wide * pack), jnp.bfloat16),
             pltpu.VMEM((n * piece, wide), jnp.bfloat16),
             pltpu.VMEM((n, rows, 2 * wide), jnp.bfloat16),
         ]
@@ -370,7 +384,7 @@
         in_specs=[smem, vmem, vmem],
         out_specs=(vmem, vmem),
         scratch_shapes=[pltpu.VMEM((AB * BS, wide), jnp.float32)],
-        compiler_params=pltpu.CompilerParams(vmem_limit_bytes=32 * 1024 * 1024),
+        compiler_params=pltpu.CompilerParams(vmem_limit_bytes=62 * 1024 * 1024),
     )(all_ids, blocks, images)
     return gram, applied.T
 

time: 35.3 us -> 33 us (0.935)
  local copies, waits for them, and re-layouts: 2.24 us -> 0.09 us
  Pallas kernels: 31.3 us -> 30.7 us
  other arithmetic: 0.82 us -> 1.33 us
    unnamed x4 -> x0, local copies, waits for them, and re-layouts: 2.16 us -> none
    pallas_call x1, Pallas kernels: 28.1 us -> 26.8 us  [shards(): pl.pallas_call(functools.partial(exchange, n, noise_weights.shape[0]), ou...]
    pallas_call x1, Pallas kernels: 3.19 us -> 3.9 us  [shards(): pl.pallas_call(functools.partial(combine, n), out_shape=(jax.ShapeDtypeSt...]
    concatenate x1, other arithmetic: 0.08 us -> 0.58 us  [shards(): jnp.concatenate([all_ids, same[None], col[None].astype(jnp.int32)])]
where the time goes in v4:
time: 33 us; the launch traced here: 32.8 us
  Pallas kernels  30.7 us (93%)
  other arithmetic  1.33 us (4%)
  between operations  0.65 us (2%)
    pallas_call x1, Pallas kernels, shards(): pl.pallas_call(functools.partial(exchange, n, noise_weights.shape[0]), ou...  26.8 us
    pallas_call x1, Pallas kernels, shards(): pl.pallas_call(functools.partial(combine, n), out_shape=(jax.ShapeDtypeSt...  3.9 us
    convert_element_type x1, other arithmetic, shards(): blocks[:, :, 2 * rows, :2 * kept].astype(jnp.float32).astype(jnp.int32)  0.74 us

profile of v4, /device:TPU:0, one launch (start us, length us, event | category | flops | bytes accessed | tf_op | source)
XLA Modules:
  0.0 32.8 jit_solution(17966071592670652843)
XLA Ops:
  0.6 26.8 %shard_map.104 = (bf16[2,4,272,256]{3,2,1,0:T(8,128)(2,1)}, bf16[4,128,128]{2,1,0:T(8,128)(2,1)}) custom-call(bf16[128,256]{1,0:T(8,128)(2,1)} %slope_hbm.1, bf16[128,256]{1,0:T(8,128)(2,1)} %prior_hbm.1, s32[1,2]{1,0:T(1,128)} %slope_ids_hbm.1, s32[1,2]{1,0:T(1,128)} %prior_ids_hbm.1, s32[1,64]{1,0:T(1,128)} %bitcast.9, s32[1,64]{1,0:T(1,128)} %bitcast.10, ...), custom_call_target="tpu_custom_call" | custom-call | tf_op jit(solution)/shard_map/pallas_call | solution.py:345
  27.5 0.7 %convert_reduce_fusion = s32[2,4,4]{2,1,0:T(4,128)S(1)} fusion(bf16[2,4,272,256]{3,2,1,0:T(8,128)(2,1)} %get-tuple-element.6.blocks), kind=kLoop, calls=%fused_computation | loop fusion | flops 64 | bytes 192 | tf_op jit(solution)/shard_map/convert_element_type | solution.py:375
  28.2 0.1 convert_element_type.14
  28.3 0.6 %pad_add_fusion.ids_ref = s32[34]{0:T(128)} fusion(s32[1]{0:T(128)} %bitcast.6, s32[1]{0:T(128)} %bitcast.5, s32[32]{0:T(128)S(1)} %convert_element_type.14), kind=kLoop, calls=%fused_computation.1 | loop fusion | flops 68 | bytes 272 | tf_op jit(solution)/shard_map/concatenate | solution.py:377
  28.9 3.9 %shard_map.105 = (f32[768,768]{1,0:T(8,128)}, f32[64,192]{1,0:T(8,128)}) custom-call(s32[34]{0:T(128)} %pad_add_fusion.ids_ref, bf16[2,4,272,256]{3,2,1,0:T(8,128)(2,1)} %get-tuple-element.6.blocks, bf16[4,128,128]{2,1,0:T(8,128)(2,1)} %get-tuple-element.7.images), custom_call_target="tpu_custom_call" | custom-call | tf_op jit(solution)/shard_map/pallas_call | solution.py:378

commit v5 on v4

--- a/solution.py
+++ b/solution.py
@@ -189,10 +189,6 @@
 
             use(col + t)
 
-        if t < n // 2:
-            came_column(lax.rem(row + 2 * t, n)).wait_recv()
-            pass_column(t).start()
-
     step(1)
 
     @pl.when(row != col)
@@ -230,6 +226,9 @@
 
     for t in range(2, n - 1):
         step(t)
+    for m in range(1, n // 2):
+        came_column(lax.rem(row + 2 * m, n)).wait_recv()
+        pass_column(m).start()
 
     for copy in sends_v:
         copy.wait_recv()
@@ -287,14 +286,21 @@
         copy.wait_send()
 
 
-def combine(n, ids_ref, blocks, images, gram, applied, total):
+def combine(n, blocks, images, gram, applied, total, ids_wide, ids_ref, ids_sem):
     rows = images.shape[1]
     kept = blocks.shape[3] // BS
     wide = images.shape[2] // 2
-    same = ids_ref[4 * n * kept]
-    quarter = ids_ref[4 * n * kept + 1]
+    quarter = lax.axis_index("col")
+    same = jnp.where(lax.axis_index("row") == quarter, 0, 1)
+    for slot in range(2):
+        for i in range(n):
+            names = blocks[slot, i, 2 * rows:2 * rows + EXTRA, 0:BS].astype(jnp.float32)
+            ids_wide[slot * n + i:slot * n + i + 1, :] = names[0:1, :].astype(jnp.int32)
+    copy = pltpu.make_async_copy(ids_wide, ids_ref, ids_sem)
+    copy.start()
     gram[...] = jnp.zeros_like(gram)
     total[...] = jnp.zeros_like(total)
+    copy.wait()
     for i in range(n):
         for part in range(2):
             left = blocks[same, i, part * rows:(part + 1) * rows, :]
@@ -311,11 +317,11 @@
             product = lax.dot_general(left, right, over, preferred_element_type=jnp.float32)
             shown = lax.dot_general(left, image, over, preferred_element_type=jnp.float32)
             for a in range(kept):
-                down = ids_ref[(same * n + i) * 2 * kept + part * kept + a]
+                down = ids_ref[same * n + i, part * kept + a]
                 down = pl.multiple_of(down * BS, BS)
                 total[pl.ds(down, BS), :] += shown[a * BS:(a + 1) * BS]
                 for b in range(kept):
-                    across = ids_ref[i * 2 * kept + part * kept + b]
+                    across = ids_ref[i, part * kept + b]
                     across = pl.multiple_of(across * BS, BS)
                     gram[pl.ds(down, BS), pl.ds(across, BS)] += product[
                         a * BS:(a + 1) * BS, b * BS:(b + 1) * BS
@@ -328,13 +334,10 @@
     n, slope_matrix, prior_matrix, slope_blocks, prior_blocks,
     weight_ids, valid_mask, noise_weights, prior_weights, frames,
 ):
-    row = lax.axis_index("row")
-    col = lax.axis_index("col")
     rows, width = slope_matrix.shape
     kept = width // BS
     piece, wide = frames.shape
     vmem = pl.BlockSpec(memory_space=pltpu.VMEM)
-    smem = pl.BlockSpec(memory_space=pltpu.SMEM)
     tall = 2 * rows + EXTRA
     pack = 2 if piece % 32 == 0 else 1
     pairs = pltpu.SemaphoreType.DMA((n,))
@@ -372,20 +375,22 @@
         slope_matrix, prior_matrix, slope_blocks, prior_blocks, weight_ids[None], valid_mask[None],
         noise_weights[None], prior_weights[None], frames.T,
     )
-    all_ids = blocks[:, :, 2 * rows, :2 * kept].astype(jnp.float32).astype(jnp.int32).reshape(-1)
-    same = jnp.where(row == col, 0, 1).astype(jnp.int32)
-    all_ids = jnp.concatenate([all_ids, same[None], col[None].astype(jnp.int32)])
     gram, applied = pl.pallas_call(
         functools.partial(combine, n),
         out_shape=(
             jax.ShapeDtypeStruct((AB * BS, AB * BS), jnp.float32),
             jax.ShapeDtypeStruct((wide, piece), jnp.float32),
         ),
-        in_specs=[smem, vmem, vmem],
+        in_specs=[vmem, vmem],
         out_specs=(vmem, vmem),
-        scratch_shapes=[pltpu.VMEM((AB * BS, wide), jnp.float32)],
+        scratch_shapes=[
+            pltpu.VMEM((AB * BS, wide), jnp.float32),
+            pltpu.VMEM((2 * n, BS), jnp.int32),
+            pltpu.SMEM((2 * n, BS), jnp.int32),
+            pltpu.SemaphoreType.DMA,
+        ],
         compiler_params=pltpu.CompilerParams(vmem_limit_bytes=62 * 1024 * 1024),
-    )(all_ids, blocks, images)
+    )(blocks, images)
     return gram, applied.T
 
 

time: 33 us -> 30.1 us (0.912)
  Pallas kernels: 30.7 us -> 29.3 us
  other arithmetic: 1.33 us -> 0 us
    pallas_call x1, Pallas kernels: 26.8 us -> 24.7 us  [shards(): pl.pallas_call(functools.partial(exchange, n, noise_weights.shape[0]), ou...]
    convert_element_type x1 -> x0, other arithmetic: 0.74 us -> none  [shards(): blocks[:, :, 2 * rows, :2 * kept].astype(jnp.float32).astype(jnp.int32)]
    pallas_call x1, Pallas kernels: 3.9 us -> 4.57 us  [shards(): pl.pallas_call(functools.partial(combine, n), out_shape=(jax.ShapeDtypeSt...]
    concatenate x1 -> x0, other arithmetic: 0.58 us -> none  [shards(): jnp.concatenate([all_ids, same[None], col[None].astype(jnp.int32)])]
where the time goes in v5:
time: 30.1 us; the launch traced here: 29.9 us
  Pallas kernels  29.3 us (97%)
  between operations  0.64 us (2%)
    pallas_call x1, Pallas kernels, shards(): pl.pallas_call(functools.partial(exchange, n, noise_weights.shape[0]), ou...  24.7 us
    pallas_call x1, Pallas kernels, shards(): pl.pallas_call(functools.partial(combine, n), out_shape=(jax.ShapeDtypeSt...  4.57 us

profile of v5, /device:TPU:0, one launch (start us, length us, event | category | flops | bytes accessed | tf_op | source)
XLA Modules:
  0.0 29.9 jit_solution(16456842889196517977)
XLA Ops:
  0.6 24.7 %shard_map.104 = (bf16[2,4,272,256]{3,2,1,0:T(8,128)(2,1)}, bf16[4,128,128]{2,1,0:T(8,128)(2,1)}) custom-call(bf16[128,256]{1,0:T(8,128)(2,1)} %slope_hbm.1, bf16[128,256]{1,0:T(8,128)(2,1)} %prior_hbm.1, s32[1,2]{1,0:T(1,128)} %slope_ids_hbm.1, s32[1,2]{1,0:T(1,128)} %prior_ids_hbm.1, s32[1,64]{1,0:T(1,128)} %bitcast.7, s32[1,64]{1,0:T(1,128)} %bitcast.8, ...), custom_call_target="tpu_custom_call" | custom-call | tf_op jit(solution)/shard_map/pallas_call | solution.py:348
  25.4 4.6 %shard_map.105 = (f32[768,768]{1,0:T(8,128)}, f32[64,192]{1,0:T(8,128)}) custom-call(bf16[2,4,272,256]{3,2,1,0:T(8,128)(2,1)} %get-tuple-element.6.blocks, bf16[4,128,128]{2,1,0:T(8,128)(2,1)} %get-tuple-element.7.images), custom_call_target="tpu_custom_call" | custom-call | tf_op jit(solution)/shard_map/pallas_call | solution.py:378
